TPU v7x, 32 devices: a whole 2x2x4 slice. The times are simulated.
32 devices in a mesh: groups: 2 (over x), seg: 16 (over z, y, core).
Axes of the slice: x: 2, y: 2, z: 4, core: 2. Of those that a mesh axis runs over, the one named last changes fastest.
Arguments:
- hidden: bfloat16 [1024, 28672], P(('groups', 'seg')), parts along dimension 0, may hold values from -6 to 6
- base_down_matrix: bfloat16 [28672, 8192], P('seg'), may hold values from -0.03125 to 0.03125
- adapter_shrink_blocks: bfloat16 [16, 28672, 128], P('seg'), may hold values from -0.03125 to 0.03125
- adapter_expand_blocks: bfloat16 [16, 128, 8192], P('seg'), may hold values from -0.5 to 0.5
- row_adapter_index: int32 [1024, 1], P(('groups', 'seg')), parts along dimension 0, may hold values from 0 to 15; in each aligned block of 32 rows (0 to 31, 32 to 63, ...) at most 2 rows name the same one
- adapter_storage_slot: int32 [16], replicated, may hold values from 0 to 15, each once
Outputs:
- output: bfloat16 [1024, 8192], P(('groups', 'seg')), parts along dimension 0
There are 2 independent parts, one for each index of `groups`. A program takes and returns all parts, laid end to end along the dimension named above; an argument that names none is the same for every part. Nothing has to cross between parts.
Inputs may be any that keep to these rules, and one draw needn't show every extreme that they name: `row_adapter_index`: within the rows of one device no adapter is named more than 2 times, and in every draw some adapter is named exactly 2 times on some device. Each storage slot is used by exactly one adapter; adapter a's blocks are adapter_shrink_blocks[adapter_storage_slot[a]] and adapter_expand_blocks[adapter_storage_slot[a]].
All inputs are finite; a program needn't handle non-finite values.
Results may differ from a plain program's by a relative error of at most 0.005.
Values may be sent and summed in bfloat16 or wider, within the bound.
A program may use at most 192 MiB of HBM per device.

v0:
```python
import jax
import jax.numpy as jnp
from jax import lax
from jax.sharding import PartitionSpec as P

MOST = 2


def local(
    hidden,
    base_down_matrix,
    adapter_shrink_blocks,
    adapter_expand_blocks,
    row_adapter_index,
    adapter_storage_slot,
):
    peer_count = lax.axis_size("seg")
    row_count = hidden.shape[0]
    width = base_down_matrix.shape[1]
    ff_width = hidden.shape[1]
    slot_count = peer_count * MOST
    feature_rows = lax.all_to_all(hidden, "seg", split_axis=1, concat_axis=0, tiled=True)
    adapter_of = row_adapter_index[:, 0]
    table_size = adapter_storage_slot.shape[0]
    owner_of = jnp.sum(
        jnp.where(
            adapter_of[:, None] == jnp.arange(table_size, dtype=jnp.int32)[None, :],
            adapter_storage_slot[None, :],
            0,
        ),
        axis=1,
    )
    row_index = jnp.arange(row_count, dtype=jnp.int32)
    earlier = jnp.sum(
        (
            (adapter_of[:, None] == adapter_of[None, :]) & (row_index[None, :] < row_index[:, None])
        ).astype(jnp.int32),
        axis=1,
    )
    position = owner_of * MOST + earlier
    one_hot = position[None, :] == jnp.arange(slot_count, dtype=jnp.int32)[:, None]
    send_rows = jnp.dot(
        one_hot.astype(jnp.bfloat16), hidden, preferred_element_type=jnp.float32
    ).astype(jnp.bfloat16)
    send_rows = send_rows.reshape(peer_count, MOST, ff_width)
    shrink_weight_block = adapter_shrink_blocks[0]
    expand_weight_block = adapter_expand_blocks[0]
    slot_rows = lax.all_to_all(send_rows, "seg", split_axis=0, concat_axis=0, tiled=True)
    sources = slot_rows.shape[0]
    items = slot_rows.shape[1]
    flat = slot_rows.reshape(sources * items, ff_width)
    shrunk = jnp.dot(flat, shrink_weight_block, preferred_element_type=jnp.float32).astype(
        jnp.bfloat16
    )
    update = jnp.dot(shrunk, expand_weight_block, preferred_element_type=jnp.float32).astype(
        jnp.bfloat16
    )
    came_back = lax.all_to_all(
        update.reshape(sources, items, width), "seg", split_axis=0, concat_axis=0, tiled=True
    )
    row_update = jnp.take(came_back.reshape(slot_count, width), position, axis=0)
    base_rows = lax.psum_scatter(
        jnp.dot(feature_rows, base_down_matrix, preferred_element_type=jnp.float32),
        "seg",
        scatter_dimension=0,
        tiled=True,
    )
    output = (base_rows + row_update.astype(jnp.float32)).astype(jnp.bfloat16)
    return output


def solution(mesh):
    return jax.shard_map(
        local,
        mesh=mesh,
        in_specs=(
            P(("groups", "seg"), None),
            P("seg", None),
            P("seg", None, None),
            P("seg", None, None),
            P(("groups", "seg"), None),
            P(),
        ),
        out_specs=P(("groups", "seg"), None),
        check_vma=False,
    )
```

profile of v0, /device:TPU:0, one launch (start us, length us, event | category | flops | bytes accessed | tf_op | source)
XLA Modules:
  0.0 298.6 jit_solution(10777276538677016473)
XLA Ops:
  6.5 0.0 copy-start
  6.5 0.0 reduce-scatter.2.cloned.1.call-start
  6.5 1.8 copy.12
  8.4 49.9 %all_to_all.29 = bf16[32,16,1792]{2,0,1:T(8,128)(2,1)S(1)} all-to-all(bf16[32,16,1792]{2,0,1:T(8,128)(2,1)S(1)} %bitcast.26), channel_id=1, replica_groups=mesh['groups'=2,'seg'=16] {'seg'}, dimensions={1} | all-to-all | bytes 3670016 | tf_op jit(solution)/shard_map/all_to_all | solution.py:22
  58.3 24.1 %fusion.11 = f32[512,8192]{1,0:T(8,128)} fusion(bf16[512,1792]{1,0:T(8,128)(2,1)S(1)} %bitcast.28, bf16[1792,8192]{1,0:T(8,128)(2,1)} %param.7), kind=kOutput, calls=%fused_computation.22 | convolution fusion | flops 15032385536 | bytes 47972352 | tf_op jit(solution)/shard_map/dot_general | solution.py:63
  82.4 0.0 copy-start.1
  82.4 0.0 copy-start.2
  82.4 0.0 reduce-scatter.2.cloned.1.call-update
  82.4 0.6 copy-done.1
  83.1 0.2 convert_reduce_fusion
  83.2 0.0 copy-done.2
  83.2 0.1 select_reduce_fusion
  83.3 3.4 %convolution_convert_fusion = bf16[32,28672]{1,0:T(8,128)(2,1)} fusion(bf16[32,28672]{1,0:T(8,128)(2,1)} %param.6, s32[32]{0:T(128)S(1)} %get-tuple-element.6), kind=kOutput, calls=%fused_computation.1 | convolution fusion | flops 59638784 | bytes 3670144 | tf_op jit(solution)/shard_map/dot_general | solution.py:42
  86.7 3.6 %reshape.55 = bf16[16,2,28672]{2,1,0:T(2,128)(2,1)} reshape(bf16[32,28672]{1,0:T(8,128)(2,1)} %convolution_convert_fusion) | data formatting | bytes 3670016 | tf_op jit(solution)/shard_map/reshape | solution.py:45
  90.3 71.0 %all_to_all.30 = bf16[16,2,28672]{2,1,0:T(2,128)(2,1)} all-to-all(bf16[16,2,28672]{2,1,0:T(2,128)(2,1)} %reshape.55), channel_id=1, replica_groups=mesh['groups'=2,'seg'=16] {'seg'}, dimensions={0} | all-to-all | bytes 3670016 | tf_op jit(solution)/shard_map/all_to_all | solution.py:48
  161.2 2.8 reshape.56
  164.1 0.0 copy-done
  164.1 5.3 %convolution_convert_fusion.1 = bf16[32,8192]{1,0:T(8,128)(2,1)S(1)} fusion(bf16[1,128,8192]{2,1,0:T(8,128)(2,1)S(1)} %copy-done, bf16[32,28672]{1,0:T(8,128)(2,1)} %reshape.56, bf16[1,28672,128]{2,1,0:T(8,128)(2,1)} %param.8), kind=kOutput, calls=%fused_computation.2 | convolution fusion | flops 302256128 | bytes 11796480 | tf_op jit(solution)/shard_map/dot_general | solution.py:55
  169.4 1.1 reshape.57
  170.5 7.4 %all-to-all-start.2 = ((bf16[16,2,8192]{2,1,0:T(2,128)(2,1)}), bf16[16,2,8192]{2,1,0:T(2,128)(2,1)S(1)}, u32[]{:S(2)}, u32[]{:S(2)}) async-start(bf16[16,2,8192]{2,1,0:T(2,128)(2,1)} %reshape.57), calls=%async_computation.3 | async-start | bytes 1048576 | tf_op jit(solution)/shard_map/all_to_all | solution.py:58
  177.9 23.1 %all-to-all-done.2 = bf16[16,2,8192]{2,1,0:T(2,128)(2,1)S(1)} async-done(((bf16[16,2,8192]{2,1,0:T(2,128)(2,1)}), bf16[16,2,8192]{2,1,0:T(2,128)(2,1)S(1)}, u32[]{:S(2)}, u32[]{:S(2)}) %all-to-all-start.2) | async-done | bytes 524320 | tf_op jit(solution)/shard_map/all_to_all | solution.py:58
  201.0 0.2 reshape.58
  201.2 0.9 gather_fusion
  202.1 87.5 %reduce-scatter.2.cloned.1.call-done = f32[32,8192]{1,0:T(8,128)} async-done(((f32[512,8192]{1,0:T(8,128)}), f32[32,8192]{1,0:T(8,128)}) %reduce-scatter.2.cloned.1.call-update) | async-done | bytes 1048592 | tf_op jit(solution)/shard_map/reduce_scatter | solution.py:62
  289.6 2.2 add_convert_fusion
  (3 shorter events, 0.0 us)
Async XLA Ops:
  6.5 157.5 %copy-start = (bf16[1,128,8192]{2,1,0:T(8,128)(2,1)S(1)}, bf16[1,128,8192]{2,1,0:T(8,128)(2,1)}, u32[]{:S(2)}) copy-start(bf16[1,128,8192]{2,1,0:T(8,128)(2,1)} %param.9) | copy-start | bytes 6291460
  6.5 283.0 %reduce-scatter.2.cloned.1.call-start = ((), (), s32[]{:S(2)}) async-start(), calls=%async_computation.4 | async-start | bytes 17825792 | tf_op jit(solution)/shard_map/reduce_scatter | solution.py:62
  82.4 0.7 copy-start.1
  82.4 0.8 copy-start.2
  170.5 30.5 %all-to-all-start.2 = ((bf16[16,2,8192]{2,1,0:T(2,128)(2,1)}), bf16[16,2,8192]{2,1,0:T(2,128)(2,1)S(1)}, u32[]{:S(2)}, u32[]{:S(2)}) async-start(bf16[16,2,8192]{2,1,0:T(2,128)(2,1)} %reshape.57), calls=%async_computation.3 | async-start | bytes 1048576 | tf_op jit(solution)/shard_map/all_to_all | solution.py:58
Sparse Core Ops, SparseCore 0:
  82.5 206.9 reduce-scatter.1
where the time goes:
time: 299 us
  blocking collectives  121 us (40%)
  waiting for transfers between devices  111 us (37%)
  matrix products  32.7 us (11%)
  between operations  13.5 us (5%)
  local copies, waits for them, and re-layouts  11.1 us (4%)
  starting transfers between devices  7.4 us (2%)
    reduce_scatter x1, waiting for transfers between devices, local(): lax.psum_scatter(jnp.dot(feature_rows, base_down_matrix, preferred_elemen...  87.5 us
    all_to_all x1, blocking collectives, local(): lax.all_to_all(send_rows, 'seg', split_axis=0, concat_axis=0, tiled=True)  71 us
    all_to_all x1, blocking collectives, local(): lax.all_to_all(hidden, 'seg', split_axis=1, concat_axis=0, tiled=True)  49.9 us
    dot_general x1, matrix products, local(): jnp.dot(feature_rows, base_down_matrix, preferred_element_type=jnp.float32)  24.1 us
    all_to_all x1, waiting for transfers between devices, local(): lax.all_to_all(update.reshape(sources, items, width), 'seg', split_axis=0...  23.1 us
    all_to_all x1, starting transfers between devices, local(): lax.all_to_all(update.reshape(sources, items, width), 'seg', split_axis=0...  7.39 us
  transfers between devices with their start and end apart: 2, of which 2 were waited for; matrix products, arithmetic and copies ran while one was open for 6% of the time, Pallas kernels for 0%

commit v1 on v0

v1 whole, which is shorter than its diff:
```python
import functools

import jax
import jax.numpy as jnp
from jax import lax
from jax.experimental import pallas as pl
from jax.experimental.pallas import tpu as pltpu
from jax.sharding import PartitionSpec as P

MOST = 2
TILE = 16
PIECES = TILE // MOST
LANES = 128
SLOTS = 4
LAG = 2
MESH = pl.DeviceIdType.MESH


def reversed_bits(value, bits):
    return sum(((value >> b) & 1) << (bits - 1 - b) for b in range(bits))


def partner_of(me, offset, bits):
    for b in range(bits):
        if (offset >> b) & 1:
            me = me + (1 - 2 * ((me // (1 << b)) % 2)) * (1 << b)
    return me


def kernel(n, bits, chunk, rows, message_ref, hidden_ref, base_ref, shrink_ref, expand_ref, out_ref,
           features, messages, shrink, expand, base, spread, shrunk, *rest):
    keeps, sends, recvs = rest[:bits], rest[bits:2 * bits], rest[2 * bits:3 * bits]
    send_sems, recv_sems = rest[3 * bits:4 * bits], rest[4 * bits:5 * bits]
    base_sem, weight_sem, own_sem, message_send, message_recv, hidden_send, hidden_recv = rest[5 * bits:]
    me = lax.axis_index("seg")
    depth = base_ref.shape[0]
    steps = base_ref.shape[1] // chunk
    piece = messages.shape[1] - LANES
    slot_count = n * MOST

    def base_copy(i, slot):
        columns = pl.ds(pl.multiple_of(i * chunk, chunk), chunk)
        return pltpu.make_async_copy(base_ref.at[:, columns], base.at[slot], base_sem.at[slot])

    shrink_copy = pltpu.make_async_copy(shrink_ref.at[0], shrink, weight_sem.at[0])
    expand_copy = pltpu.make_async_copy(expand_ref.at[0], expand, weight_sem.at[1])
    own_message = pltpu.make_async_copy(
        message_ref.at[pl.ds(pl.multiple_of(me * TILE, TILE), TILE), :], messages.at[pl.ds(0, TILE), :], own_sem.at[0])
    own_hidden = pltpu.make_async_copy(
        hidden_ref.at[:, pl.ds(pl.multiple_of(me * depth, LANES), depth)], features.at[pl.ds(0, rows), :], own_sem.at[1])

    barrier = pltpu.get_barrier_semaphore()
    for k in range(1, n):
        pl.semaphore_signal(barrier, inc=1, device_id={"seg": partner_of(me, k, bits)}, device_id_type=MESH)
    shrink_copy.start()
    expand_copy.start()
    own_message.start()
    own_hidden.start()
    for i in range(SLOTS):
        base_copy(i, i).start()
    pl.semaphore_wait(barrier, n - 1)

    message_copies, hidden_copies = [], []
    for k in range(n - 1, 0, -1):
        to, place = partner_of(me, k, bits), reversed_bits(k, bits)
        message_copies.append(pltpu.make_async_remote_copy(
            src_ref=message_ref.at[pl.ds(pl.multiple_of(to * TILE, TILE), TILE), :],
            dst_ref=messages.at[pl.ds(place * TILE, TILE), :],
            send_sem=message_send.at[k], recv_sem=message_recv.at[k],
            device_id={"seg": to}, device_id_type=MESH))
        hidden_copies.append(pltpu.make_async_remote_copy(
            src_ref=hidden_ref.at[:, pl.ds(pl.multiple_of(to * depth, LANES), depth)],
            dst_ref=features.at[pl.ds(place * rows, rows), :],
            send_sem=hidden_send.at[k], recv_sem=hidden_recv.at[k],
            device_id={"seg": to}, device_id_type=MESH))
    for copy in message_copies:
        copy.start()
    for copy in hidden_copies:
        copy.start()

    shrink_copy.wait()
    expand_copy.wait()
    own_message.wait()
    for copy in message_copies:
        copy.wait()

    piece_of = lax.broadcasted_iota(jnp.int32, (slot_count * PIECES, LANES), 0) & (PIECES - 1)

    def shrink_piece(p, total):
        part = jnp.dot(messages[:, pl.ds(0, piece)], shrink[pl.ds(pl.multiple_of(p * piece, LANES), piece), :],
                       preferred_element_type=jnp.float32)
        return total + jnp.where(piece_of == p, part, 0.0)

    total = lax.fori_loop(0, PIECES, shrink_piece, jnp.zeros((slot_count * PIECES, LANES), jnp.float32))
    shrunk[...] = jnp.sum(total.reshape(slot_count, PIECES, LANES), axis=1).astype(jnp.bfloat16)
    tags = messages[:, pl.ds(piece, LANES)].astype(jnp.float32).reshape(slot_count, PIECES, LANES)
    tags = jnp.concatenate([jnp.max(tags, axis=1)] * (n * rows // LANES), axis=1)
    tags = jnp.where(
        lax.broadcasted_iota(jnp.int32, tags.shape, 0) // MOST == lax.broadcasted_iota(jnp.int32, tags.shape, 1) // rows,
        tags, 0.0)
    spread[...] = jnp.transpose(tags).astype(jnp.bfloat16)

    own_hidden.wait()
    for copy in hidden_copies:
        copy.wait()

    def sum_copy(stage, i):
        slot = i % SLOTS
        return pltpu.make_async_remote_copy(
            src_ref=sends[stage].at[slot], dst_ref=recvs[stage].at[i],
            send_sem=send_sems[stage].at[slot], recv_sem=recv_sems[stage].at[i],
            device_id={"seg": partner_of(me, 1 << stage, bits)}, device_id_type=MESH)

    def pass_on(stage, i, value):
        half = value.shape[0] // 2
        slot = i % SLOTS

        @pl.when(i >= SLOTS)
        def _():
            sum_copy(stage, i - SLOTS).wait_send()

        sends[stage][slot] = value[half:].astype(jnp.bfloat16)
        sum_copy(stage, i).start()
        keeps[stage][slot] = value[:half]

    def received(stage, i):
        sum_copy(stage, i).wait_recv()
        return keeps[stage][i % SLOTS] + recvs[stage][i].astype(jnp.float32)

    behind = [0] + [1 + LAG * s for s in range(bits)]

    def step(i, carry):
        @pl.when(i < steps)
        def _():
            slot = i % SLOTS
            base_copy(i, slot).wait()
            columns = pl.ds(pl.multiple_of(i * chunk, chunk), chunk)
            update = jnp.dot(shrunk[...], expand[:, columns], preferred_element_type=jnp.float32).astype(jnp.bfloat16)
            value = jnp.dot(features[...], base[slot], preferred_element_type=jnp.float32)
            value = value + jnp.dot(spread[...], update, preferred_element_type=jnp.float32)
            pass_on(0, i, value)

            @pl.when(i + SLOTS < steps)
            def _():
                base_copy(i + SLOTS, slot).start()

        for stage in range(1, bits + 1):
            j = i - behind[stage]

            @pl.when((j >= 0) & (j < steps))
            def _():
                value = received(stage - 1, j)
                if stage < bits:
                    pass_on(stage, j, value)
                else:
                    out_ref[:, pl.ds(pl.multiple_of(j * chunk, chunk), chunk)] = value.astype(out_ref.dtype)

        return carry

    lax.fori_loop(0, steps + behind[-1], step, 0)
    for stage in range(bits):
        for i in range(max(0, steps - SLOTS), steps):
            sum_copy(stage, i).wait_send()


def local(hidden, base_down_matrix, adapter_shrink_blocks, adapter_expand_blocks, row_adapter_index,
          adapter_storage_slot):
    n = lax.axis_size("seg")
    bits = n.bit_length() - 1
    rows, ff_width = hidden.shape
    depth, width = base_down_matrix.shape
    rank = adapter_shrink_blocks.shape[2]
    slot_count = n * MOST
    piece = ff_width // PIECES
    chunk = min(512, width // SLOTS)
    steps = width // chunk

    adapter_of = row_adapter_index[:, 0]
    table_size = adapter_storage_slot.shape[0]
    owner_of = jnp.sum(
        jnp.where(adapter_of[:, None] == jnp.arange(table_size, dtype=jnp.int32)[None, :],
                  adapter_storage_slot[None, :], 0), axis=1)
    row_index = jnp.arange(rows, dtype=jnp.int32)
    earlier = jnp.sum(
        ((adapter_of[:, None] == adapter_of[None, :]) & (row_index[None, :] < row_index[:, None])).astype(jnp.int32),
        axis=1)
    position = owner_of * MOST + earlier
    line = jnp.arange(slot_count * PIECES, dtype=jnp.int32)
    source = jnp.arange(PIECES * rows, dtype=jnp.int32)
    pick = (jnp.tile(position, PIECES)[None, :] == (line // PIECES)[:, None]) & (
        (source // rows)[None, :] == (line % PIECES)[:, None])
    pieces = hidden.reshape(rows, PIECES, piece).transpose(1, 0, 2).reshape(PIECES * rows, piece)
    tag = ((source % rows)[:, None] == (jnp.arange(LANES, dtype=jnp.int32) % rows)[None, :]).astype(jnp.bfloat16)
    message = jnp.dot(pick.astype(jnp.bfloat16), jnp.concatenate([pieces, tag], axis=1),
                      preferred_element_type=jnp.float32).astype(jnp.bfloat16)

    halves = [n * rows >> (s + 1) for s in range(bits)]
    anywhere = pl.BlockSpec(memory_space=pl.ANY)
    return pl.pallas_call(
        functools.partial(kernel, n, bits, chunk, rows),
        out_shape=jax.ShapeDtypeStruct((rows, width), jnp.bfloat16),
        in_specs=[anywhere] * 5,
        out_specs=pl.BlockSpec(memory_space=pltpu.VMEM),
        scratch_shapes=[
            pltpu.VMEM((n * rows, depth), jnp.bfloat16),
            pltpu.VMEM((n * TILE, piece + LANES), jnp.bfloat16),
            pltpu.VMEM((ff_width, rank), jnp.bfloat16),
            pltpu.VMEM((rank, width), jnp.bfloat16),
            pltpu.VMEM((SLOTS, depth, chunk), jnp.bfloat16),
            pltpu.VMEM((n * rows, slot_count), jnp.bfloat16),
            pltpu.VMEM((slot_count, rank), jnp.bfloat16),
            *[pltpu.VMEM((SLOTS, h, chunk), jnp.float32) for h in halves],
            *[pltpu.VMEM((SLOTS, h, chunk), jnp.bfloat16) for h in halves],
            *[pltpu.VMEM((steps, h, chunk), jnp.bfloat16) for h in halves],
            *[pltpu.SemaphoreType.DMA((SLOTS,)) for _ in halves],
            *[pltpu.SemaphoreType.DMA((steps,)) for _ in halves],
            pltpu.SemaphoreType.DMA((SLOTS,)),
            pltpu.SemaphoreType.DMA((2,)),
            pltpu.SemaphoreType.DMA((2,)),
            *[pltpu.SemaphoreType.DMA((n,)) for _ in range(4)],
        ],
        compiler_params=pltpu.CompilerParams(
            collective_id=0, has_side_effects=True, vmem_limit_bytes=58 * 1024 * 1024),
        cost_estimate=pl.CostEstimate(
            flops=2 * n * rows * depth * width, bytes_accessed=2 * depth * width, transcendentals=0),
    )(message, hidden, base_down_matrix, adapter_shrink_blocks, adapter_expand_blocks)


def solution(mesh):
    return jax.shard_map(
        local,
        mesh=mesh,
        in_specs=(
            P(("groups", "seg"), None),
            P("seg", None),
            P("seg", None, None),
            P("seg", None, None),
            P(("groups", "seg"), None),
            P(),
        ),
        out_specs=P(("groups", "seg"), None),
        check_vma=False,
    )
```

time: 299 us -> 158 us (0.53)
  Pallas kernels: 0 us -> 150 us
  blocking collectives: 121 us -> 0 us
  waiting for transfers between devices: 111 us -> 0 us
  matrix products: 32.7 us -> 2.01 us
  between operations: 13.5 us -> 0.06 us
  starting transfers between devices: 7.4 us -> 0 us
  local copies, waits for them, and re-layouts: 11.1 us -> 4.53 us
    pallas_call x0 -> x1, Pallas kernels: none -> 150 us  [local(): pl.pallas_call(functools.partial(kernel, n, bits, chunk, rows), out_shape...]
    all_to_all x2 -> x0, blocking collectives: 121 us -> none  [the longest x1 71 us: local(): lax.all_to_all(send_rows, 'seg', split_axis=0, concat_axis=0, tiled=True)]
    reduce_scatter x1 -> x0, waiting for transfers between devices: 87.5 us -> none  [local(): lax.psum_scatter(jnp.dot(feature_rows, base_down_matrix, preferred_elemen...]
    dot_general x3 -> x1, matrix products: 32.7 us -> 2.01 us  [local(): jnp.dot(pick.astype(jnp.bfloat16), jnp.concatenate([pieces, tag], axis=1)...]
    all_to_all x1 -> x0, waiting for transfers between devices: 23.1 us -> none  [local(): lax.all_to_all(update.reshape(sources, items, width), 'seg', split_axis=0...]
    reshape x4 -> x0, local copies, waits for them, and re-layouts: 7.77 us -> none  [the longest x1 3.58 us: local(): send_rows = send_rows.reshape(peer_count, MOST, ff_width)]
    all_to_all x1 -> x0, starting transfers between devices: 7.39 us -> none  [local(): lax.all_to_all(update.reshape(sources, items, width), 'seg', split_axis=0...]
    unnamed x6 -> x2, local copies, waits for them, and re-layouts: 0.64 us -> 3.91 us
  transfers between devices with their start and end apart: 2 -> 0, of which waited for: 2 -> 0; matrix products, arithmetic and copies ran while one was open for 6% -> 0% of each run, Pallas kernels for 0% -> 0%
where the time goes in v1:
time: 158 us
  Pallas kernels  150 us (95%)
  local copies, waits for them, and re-layouts  4.53 us (3%)
  matrix products  2.01 us (1%)
  other arithmetic  1.79 us (1%)
    pallas_call x1, Pallas kernels, local(): pl.pallas_call(functools.partial(kernel, n, bits, chunk, rows), out_shape...  150 us
    unnamed x2, local copies, waits for them, and re-layouts  3.91 us

profile of v1, /device:TPU:0, one launch (start us, length us, event | category | flops | bytes accessed | tf_op | source)
XLA Modules:
  0.0 158.1 jit_solution(17980153719584516172)
XLA Ops:
  0.0 0.9 convert_reduce_fusion
  0.9 0.8 select_reduce_fusion
  1.7 0.1 eq.81
  1.8 0.1 compare_convert_fusion
  1.9 2.0 %copy.9 = bf16[4,8,8,3584]{3,2,1,0:T(8,128)(2,1)S(1)} copy(bf16[4,8,8,3584]{3,1,2,0:T(8,128)(2,1)} %bitcast.7) | data formatting | bytes 3670016
  4.0 0.5 copy.8
  4.5 2.0 %convolution_convert_fusion.message_ref = bf16[256,3712]{1,0:T(8,128)(2,1)} fusion(bf16[256,128]{1,0:T(8,128)(2,1)S(1)} %compare_convert_fusion, bf16[256,3584]{1,0:T(8,128)(2,1)S(1)} %bitcast.8, s32[256]{0:T(256)S(1)} %get-tuple-element.6, s32[256]{0:T(256)S(1)} %eq.81, s32[256]{0:T(256)S(1)} %get-tuple-element.5, s32[256]{0:T(256)S(1)} %and_select_fusion.4), kind=kOutput, calls=%fused_computation | convolution fusion | flops 491487232 | bytes 3805184 | tf_op jit(solution)/shard_map/dot_general | solution.py:194
  6.5 149.7 %shard_map.64 = bf16[32,8192]{1,0:T(8,128)(2,1)} custom-call(bf16[256,3712]{1,0:T(8,128)(2,1)} %convolution_convert_fusion.message_ref, bf16[32,28672]{1,0:T(8,128)(2,1)} %hidden_ref.1, bf16[1792,8192]{1,0:T(8,128)(2,1)} %base_ref.1, bf16[1,28672,128]{2,1,0:T(8,128)(2,1)} %shrink_ref.1, bf16[1,128,8192]{2,1,0:T(8,128)(2,1)} %expand_ref.1), custom_call_target="tpu_custom_call" | custom-call | flops 15032385536 | bytes 29360128 | tf_op jit(solution)/shard_map/pallas_call | solution.py:199
  156.2 1.9 %copy.11 = bf16[32,8192]{1,0:T(8,128)(2,1)} copy(bf16[32,8192]{1,0:T(8,128)(2,1)} %shard_map.64) | data formatting | bytes 1048576
  (6 shorter events, 0.0 us)

commit v2 on v1

v2 whole, which is shorter than its diff:
```python
import functools

import jax
import jax.numpy as jnp
from jax import lax
from jax.experimental import pallas as pl
from jax.experimental.pallas import tpu as pltpu
from jax.sharding import PartitionSpec as P

MOST = 2
TILE = 16
PIECES = TILE // MOST
LANES = 128
SLOTS = 4
LAG = 2
CHUNK = 512
FILL = 2
EARLY = False
AFTER = -4
MESH = pl.DeviceIdType.MESH


def reversed_bits(value, bits):
    return sum(((value >> b) & 1) << (bits - 1 - b) for b in range(bits))


def partner_of(me, offset, bits):
    for b in range(bits):
        if (offset >> b) & 1:
            me = me + (1 - 2 * ((me // (1 << b)) % 2)) * (1 << b)
    return me


def kernel(n, bits, chunk, rows, pick_ref, place_ref, hidden_ref, base_ref, shrink_ref, expand_ref, out_ref,
           features, pieces, outbox, messages, shrink, expand, base, updates, returned, base_rows, *rest):
    keeps, sends, recvs = rest[:bits], rest[bits:2 * bits], rest[2 * bits:3 * bits]
    send_sems, recv_sems = rest[3 * bits:4 * bits], rest[4 * bits:5 * bits]
    base_sem, weight_sem, own_sem, piece_sem = rest[5 * bits:5 * bits + 4]
    message_send, message_recv, hidden_send, hidden_recv, return_send, return_recv = rest[5 * bits + 4:]
    me = lax.axis_index("seg")
    depth = base_ref.shape[0]
    steps = base_ref.shape[1] // chunk
    piece = messages.shape[1]
    span = updates.shape[1]
    slot_count = n * MOST

    def base_copy(i, slot):
        columns = pl.ds(pl.multiple_of(i * chunk, chunk), chunk)
        return pltpu.make_async_copy(base_ref.at[:, columns], base.at[slot], base_sem.at[slot])

    weight_copies = []
    for p in range(PIECES):
        weight_copies.append(pltpu.make_async_copy(
            shrink_ref.at[0, pl.ds(p * piece, piece), :],
            shrink.at[pl.ds(p // 2 * piece, piece), pl.ds(p % 2 * LANES, LANES)], weight_sem.at[0, p]))
        weight_copies.append(pltpu.make_async_copy(
            expand_ref.at[0, :, pl.ds(p * span, span)], expand.at[pl.ds(p * LANES, LANES), :], weight_sem.at[1, p]))
    piece_copies = [
        pltpu.make_async_copy(hidden_ref.at[:, pl.ds(p * piece, piece)], pieces.at[pl.ds(p * rows, rows), :], piece_sem.at[p])
        for p in range(PIECES)]
    own_hidden = pltpu.make_async_copy(
        hidden_ref.at[:, pl.ds(pl.multiple_of(me * depth, LANES), depth)], features.at[pl.ds(0, rows), :], own_sem.at[0])

    barrier = pltpu.get_barrier_semaphore()
    for k in range(1, n):
        pl.semaphore_signal(barrier, inc=1, device_id={"seg": partner_of(me, k, bits)}, device_id_type=MESH)
    for copy in piece_copies:
        copy.start()
    own_hidden.start()
    pl.semaphore_wait(barrier, n - 1)

    message_copies, hidden_copies, return_copies = [], [], []
    for k in range(n - 1, 0, -1):
        to, place = partner_of(me, k, bits), reversed_bits(k, bits)
        theirs, mine = pl.ds(pl.multiple_of(to * TILE, TILE), TILE), pl.ds(pl.multiple_of(me * TILE, TILE), TILE)
        message_copies.append(pltpu.make_async_remote_copy(
            src_ref=outbox.at[theirs, :], dst_ref=messages.at[pl.ds(k * TILE, TILE), :],
            send_sem=message_send.at[k], recv_sem=message_recv.at[k],
            device_id={"seg": to}, device_id_type=MESH))
        return_copies.append(pltpu.make_async_remote_copy(
            src_ref=updates.at[pl.ds(k * TILE, TILE), :], dst_ref=returned.at[mine, :],
            send_sem=return_send.at[k], recv_sem=return_recv.at[k],
            device_id={"seg": to}, device_id_type=MESH))
        hidden_copies.append(pltpu.make_async_remote_copy(
            src_ref=hidden_ref.at[:, pl.ds(pl.multiple_of(to * depth, LANES), depth)],
            dst_ref=features.at[pl.ds(place * rows, rows), :],
            send_sem=hidden_send.at[k], recv_sem=hidden_recv.at[k],
            device_id={"seg": to}, device_id_type=MESH))
    for copy in hidden_copies:
        copy.start()
    for i in range(SLOTS):
        base_copy(i, i).start()
    for copy in weight_copies:
        copy.start()

    for copy in piece_copies:
        copy.wait()
    part = piece // FILL

    def fill(c, carry):
        columns = pl.ds(pl.multiple_of(c * part, LANES), part)
        outbox[:, columns] = jnp.dot(
            pick_ref[...], pieces[:, columns], preferred_element_type=jnp.float32).astype(jnp.bfloat16)
        return carry

    lax.fori_loop(0, FILL, fill, 0)
    messages[pl.ds(0, TILE), :] = outbox[pl.ds(pl.multiple_of(me * TILE, TILE), TILE), :]

    own_hidden.wait()
    if EARLY:
        for copy in message_copies:
            copy.start()
    for copy in hidden_copies:
        copy.wait()
    if not EARLY:
        for copy in message_copies:
            copy.start()

    def adapt():
        for copy in weight_copies:
            copy.wait()
        for copy in message_copies:
            copy.wait()
        lines = slot_count * PIECES

        def piece_and_lane(width):
            piece_of = lax.broadcasted_iota(jnp.int32, (lines, width), 0) & (PIECES - 1)
            return piece_of, lax.broadcasted_iota(jnp.int32, (lines, width), 1) // LANES

        def shrink_pair(q, total):
            term = jnp.dot(messages[...], shrink[pl.ds(pl.multiple_of(q * piece, LANES), piece), :],
                           preferred_element_type=jnp.float32)
            piece_of, lane = piece_and_lane(2 * LANES)
            return total + jnp.where(piece_of == 2 * q + lane, term, 0.0)

        total = lax.fori_loop(0, PIECES // 2, shrink_pair, jnp.zeros((lines, 2 * LANES), jnp.float32))
        total = total[:, :LANES] + total[:, LANES:]
        total = jnp.sum(total.reshape(slot_count, PIECES, LANES), axis=1, keepdims=True)
        shrunk = jnp.broadcast_to(total, (slot_count, PIECES, LANES)).reshape(lines, LANES)
        piece_of, lane = piece_and_lane(PIECES * LANES)
        shrunk = jnp.where(piece_of == lane, jnp.concatenate([shrunk] * PIECES, axis=1), 0.0).astype(jnp.bfloat16)
        updates[...] = jnp.dot(shrunk, expand[...], preferred_element_type=jnp.float32).astype(jnp.bfloat16)
        returned[pl.ds(pl.multiple_of(me * TILE, TILE), TILE), :] = updates[pl.ds(0, TILE), :]
        for copy in return_copies:
            copy.start()

    def sum_copy(stage, i):
        slot = i % SLOTS
        return pltpu.make_async_remote_copy(
            src_ref=sends[stage].at[slot], dst_ref=recvs[stage].at[i],
            send_sem=send_sems[stage].at[slot], recv_sem=recv_sems[stage].at[i],
            device_id={"seg": partner_of(me, 1 << stage, bits)}, device_id_type=MESH)

    def pass_on(stage, i, value):
        half = value.shape[0] // 2
        slot = i % SLOTS

        @pl.when(i >= SLOTS)
        def _():
            sum_copy(stage, i - SLOTS).wait_send()

        sends[stage][slot] = value[half:].astype(jnp.bfloat16)
        sum_copy(stage, i).start()
        keeps[stage][slot] = value[:half]

    def received(stage, i):
        sum_copy(stage, i).wait_recv()
        return keeps[stage][i % SLOTS] + recvs[stage][i].astype(jnp.float32)

    behind = [0] + [1 + LAG * s for s in range(bits)]

    def step(i, carry):
        @pl.when(i < steps)
        def _():
            slot = i % SLOTS
            base_copy(i, slot).wait()
            value = jnp.dot(features[...], base[slot], preferred_element_type=jnp.float32)
            pass_on(0, i, value)

            @pl.when(i + SLOTS < steps)
            def _():
                base_copy(i + SLOTS, slot).start()

        for stage in range(1, bits + 1):
            j = i - behind[stage]

            @pl.when((j >= 0) & (j < steps))
            def _():
                value = received(stage - 1, j)
                if stage < bits:
                    pass_on(stage, j, value)
                else:
                    base_rows[:, pl.ds(pl.multiple_of(j * chunk, chunk), chunk)] = value

        @pl.when(i == steps + AFTER)
        def _():
            adapt()

        return carry

    lax.fori_loop(0, steps + behind[-1], step, 0)
    for copy in return_copies:
        copy.wait()
    for p in range(PIECES):
        columns = pl.ds(p * span, span)
        update = jnp.dot(place_ref[pl.ds(p * rows, rows), :], returned[...], preferred_element_type=jnp.float32)
        out_ref[:, columns] = (base_rows[:, columns] + update).astype(out_ref.dtype)
    for stage in range(bits):
        for i in range(max(0, steps - SLOTS), steps):
            sum_copy(stage, i).wait_send()


def local(hidden, base_down_matrix, adapter_shrink_blocks, adapter_expand_blocks, row_adapter_index,
          adapter_storage_slot):
    n = lax.axis_size("seg")
    bits = n.bit_length() - 1
    rows, ff_width = hidden.shape
    depth, width = base_down_matrix.shape
    rank = adapter_shrink_blocks.shape[2]
    slot_count = n * MOST
    piece = ff_width // PIECES
    chunk = min(CHUNK, width // SLOTS)
    steps = width // chunk

    adapter_of = row_adapter_index[:, 0]
    table_size = adapter_storage_slot.shape[0]
    owner_of = jnp.sum(
        jnp.where(adapter_of[:, None] == jnp.arange(table_size, dtype=jnp.int32)[None, :],
                  adapter_storage_slot[None, :], 0), axis=1)
    row_index = jnp.arange(rows, dtype=jnp.int32)
    earlier = jnp.sum(
        ((adapter_of[:, None] == adapter_of[None, :]) & (row_index[None, :] < row_index[:, None])).astype(jnp.int32),
        axis=1)
    position = owner_of * MOST + earlier
    line = jnp.arange(slot_count * PIECES, dtype=jnp.int32)
    source = jnp.arange(PIECES * rows, dtype=jnp.int32)
    spots = jnp.tile(position, PIECES)
    pick = (spots[None, :] == (line // PIECES)[:, None]) & ((source // rows)[None, :] == (line % PIECES)[:, None])
    place = (spots[:, None] == (line // PIECES)[None, :]) & ((source // rows)[:, None] == (line % PIECES)[None, :])

    halves = [n * rows >> (s + 1) for s in range(bits)]
    anywhere = pl.BlockSpec(memory_space=pl.ANY)
    return pl.pallas_call(
        functools.partial(kernel, n, bits, chunk, rows),
        out_shape=jax.ShapeDtypeStruct((rows, width), jnp.bfloat16),
        in_specs=[pl.BlockSpec(memory_space=pltpu.VMEM)] * 2 + [anywhere] * 4,
        out_specs=pl.BlockSpec(memory_space=pltpu.VMEM),
        scratch_shapes=[
            pltpu.VMEM((n * rows, depth), jnp.bfloat16),
            pltpu.VMEM((PIECES * rows, piece), jnp.bfloat16),
            pltpu.VMEM((n * TILE, piece), jnp.bfloat16),
            pltpu.VMEM((n * TILE, piece), jnp.bfloat16),
            pltpu.VMEM((ff_width // 2, 2 * rank), jnp.bfloat16),
            pltpu.VMEM((PIECES * rank, width // PIECES), jnp.bfloat16),
            pltpu.VMEM((SLOTS, depth, chunk), jnp.bfloat16),
            pltpu.VMEM((n * TILE, width // PIECES), jnp.bfloat16),
            pltpu.VMEM((n * TILE, width // PIECES), jnp.bfloat16),
            pltpu.VMEM((rows, width), jnp.float32),
            *[pltpu.VMEM((SLOTS, h, chunk), jnp.float32) for h in halves],
            *[pltpu.VMEM((SLOTS, h, chunk), jnp.bfloat16) for h in halves],
            *[pltpu.VMEM((steps, h, chunk), jnp.bfloat16) for h in halves],
            *[pltpu.SemaphoreType.DMA((SLOTS,)) for _ in halves],
            *[pltpu.SemaphoreType.DMA((steps,)) for _ in halves],
            pltpu.SemaphoreType.DMA((SLOTS,)),
            pltpu.SemaphoreType.DMA((2, PIECES)),
            pltpu.SemaphoreType.DMA((1,)),
            pltpu.SemaphoreType.DMA((PIECES,)),
            *[pltpu.SemaphoreType.DMA((n,)) for _ in range(6)],
        ],
        compiler_params=pltpu.CompilerParams(
            collective_id=0, has_side_effects=True, vmem_limit_bytes=58 * 1024 * 1024),
        cost_estimate=pl.CostEstimate(
            flops=2 * n * rows * depth * width, bytes_accessed=2 * depth * width, transcendentals=0),
    )(pick.astype(jnp.bfloat16), place.astype(jnp.bfloat16), hidden, base_down_matrix, adapter_shrink_blocks, adapter_expand_blocks)


def solution(mesh):
    return jax.shard_map(
        local,
        mesh=mesh,
        in_specs=(
            P(("groups", "seg"), None),
            P("seg", None),
            P("seg", None, None),
            P("seg", None, None),
            P(("groups", "seg"), None),
            P(),
        ),
        out_specs=P(("groups", "seg"), None),
        check_vma=False,
    )
```

time: 158 us -> 142 us (0.90)
  Pallas kernels: 150 us -> 137 us
  local copies, waits for them, and re-layouts: 4.53 us -> 1.95 us
  matrix products: 2.01 us -> 0 us
    pallas_call x1, Pallas kernels: 150 us -> 137 us  [local(): pl.pallas_call(functools.partial(kernel, n, bits, chunk, rows), out_shape...]
    unnamed x2 -> x1, local copies, waits for them, and re-layouts: 3.91 us -> 1.87 us
    dot_general x1 -> x0, matrix products: 2.01 us -> none  [local(): jnp.dot(pick.astype(jnp.bfloat16), jnp.concatenate([pieces, tag], axis=1)...]
where the time goes in v2:
time: 142 us
  Pallas kernels  137 us (96%)
  other arithmetic  2.59 us (2%)
  local copies, waits for them, and re-layouts  1.95 us (1%)
    pallas_call x1, Pallas kernels, local(): pl.pallas_call(functools.partial(kernel, n, bits, chunk, rows), out_shape...  137 us

profile of v2, /device:TPU:0, one launch (start us, length us, event | category | flops | bytes accessed | tf_op | source)
XLA Modules:
  0.0 141.9 jit_solution(7734261669515788840)
XLA Ops:
  0.0 0.9 convert_reduce_fusion
  0.9 0.8 select_reduce_fusion
  1.7 0.1 eq.92
  1.8 0.9 and_convert_fusion
  2.7 137.4 %shard_map.64 = bf16[32,8192]{1,0:T(8,128)(2,1)} custom-call(bf16[256,256]{1,0:T(8,128)(2,1)} %get-tuple-element.6.pick_ref, bf16[256,256]{1,0:T(8,128)(2,1)} %get-tuple-element.5.place_ref, bf16[32,28672]{1,0:T(8,128)(2,1)} %hidden_ref.1, bf16[1792,8192]{1,0:T(8,128)(2,1)} %base_ref.1, bf16[1,28672,128]{2,1,0:T(8,128)(2,1)} %shrink_ref.1, ...), custom_call_target="tpu_custom_call" | custom-call | flops 15032385536 | bytes 29360128 | tf_op jit(solution)/shard_map/pallas_call | solution.py:243
  140.1 1.9 %copy.8 = bf16[32,8192]{1,0:T(8,128)(2,1)} copy(bf16[32,8192]{1,0:T(8,128)(2,1)} %shard_map.64) | data formatting | bytes 1048576
  (4 shorter events, 0.0 us)
